TPU v7x, 512 devices: a whole 4x4x16 slice. The times are simulated.
512 devices in a mesh: tm: 32 (over z, core), space: 16 (over x, y).
Axes of the slice: x: 4, y: 4, z: 16, core: 2. Of those that a mesh axis runs over, the one named last changes fastest.
Arguments:
- spectrum: float32 [2048], P('space'), may hold values from 4 to 64
- coupling: float32 [256, 2048], P('tm', 'space'), may hold values from 0 to 1, as said below
- spatial_basis: bfloat16 [2048, 2048], P(None, 'space'), may hold values from -0.125 to 0.125
- noise_keys: int32 [64], replicated, may hold values from 0 to 16777215
- noise_counters: int32 [64], replicated, may hold values from 0 to 1048575
Outputs:
- samples: float32 [2048, 16384], P('space', 'tm')
Inputs may be any that keep to these rules, and one draw needn't show every extreme that they name: `coupling`: every entry lies strictly between 0 and 1.
All inputs are finite; a program needn't handle non-finite values.
Results may differ from a plain program's by a relative error of at most 0.015.
Values may be sent and summed in bfloat16 or wider, within the bound.
A program may use at most 64 MiB of HBM per device.

v0:
```python
import jax
import jax.numpy as jnp
from jax import lax
from jax.sharding import PartitionSpec as P


def copy_for_each(x, axis):
    copies = jnp.broadcast_to(x, (lax.axis_size(axis), *x.shape))
    return lax.all_to_all(copies, axis, split_axis=0, concat_axis=0, tiled=True)


def all_in_one(x, axis):
    leaves = jax.tree.leaves(x)
    order = sorted(range(len(leaves)), key=lambda k: -leaves[k].size)
    width = (1, *leaves[order[0]].shape)[-1]
    lines = [
        jnp.pad(leaves[k].reshape(-1), (0, -leaves[k].size % width)).reshape(-1, width)
        for k in order
    ]
    both, at, found = (copy_for_each(jnp.concatenate(lines), axis), 0, {})
    for k, line in zip(order, lines):
        piece = both[:, at : at + len(line)].reshape(len(both), -1)
        found[k] = piece[:, : leaves[k].size].reshape(-1, *leaves[k].shape)
        at += len(line)
    numbers = iter(range(len(leaves)))
    return jax.tree.map(lambda _: found[next(numbers)], x)


def combined_pairwise(pieces, combine):
    while len(jax.tree.leaves(pieces)[0]) > 1:
        pieces = jax.vmap(combine)(
            *(jax.tree.map(lambda part: part[side::2], pieces) for side in (0, 1))
        )
    return jax.tree.map(lambda part: part[0], pieces)


def entering(x, axis, combine, identity, reverse):
    count, mine = (lax.axis_size(axis), lax.axis_index(axis))
    passed = jnp.arange(count) > mine if reverse else jnp.arange(count) < mine

    def kept(part, zero, own):
        part = jnp.where(
            passed.reshape(-1, *(1 for _ in own.shape)), part, jnp.asarray(zero, own.dtype)
        )
        return part[::-1] if reverse else part

    pieces = all_in_one(x, axis)
    return combined_pairwise(jax.tree.map(kept, pieces, identity, x), combine)


def laid_out(parts, dim):
    lengths = list(parts.shape[1:])
    lengths[dim] *= parts.shape[0]
    return jnp.moveaxis(parts, 0, dim).reshape(lengths)


def collect(x, axis, dim):
    parts = copy_for_each(x, axis)
    return laid_out(parts, dim)


def mix_bits(state):
    state = state ^ lax.shift_right_logical(state, jnp.int32(16))
    state = state * jnp.int32(-2048144789)
    state = state ^ lax.shift_right_logical(state, jnp.int32(13))
    state = state * jnp.int32(-1028477387)
    state = state ^ lax.shift_right_logical(state, jnp.int32(16))
    return state


def unit_value(state):
    return (lax.shift_right_logical(state, jnp.int32(8)).astype(jnp.float32) + 0.5) * (
        1.0 / 16777216.0
    )


def noise_block(noise_keys, noise_counters, step_ids, mode_ids):
    seeded = noise_keys[None, :, None] * jnp.int32(668265261)
    seeded = seeded + (noise_counters[None, :, None] + step_ids[:, None, None]) * jnp.int32(
        374761393
    )
    seeded = seeded + mode_ids[None, None, :] * jnp.int32(-1640531535)
    first = mix_bits(seeded)
    second = mix_bits(first + jnp.int32(1013904223))
    radius = jnp.sqrt(-2.0 * jnp.log(unit_value(first)))
    return radius * jnp.cos(6.283185307179586 * unit_value(second))


def moebius_product(later, earlier):
    upper_left = later[0] * earlier[0] + later[1] * earlier[2]
    upper_right = later[0] * earlier[1] + later[1] * earlier[3]
    lower_left = later[2] * earlier[0] + later[3] * earlier[2]
    lower_right = later[2] * earlier[1] + later[3] * earlier[3]
    largest = jnp.maximum(
        jnp.maximum(jnp.abs(upper_left), jnp.abs(upper_right)),
        jnp.maximum(jnp.abs(lower_left), jnp.abs(lower_right)),
    )
    return (
        upper_left / largest,
        upper_right / largest,
        lower_left / largest,
        lower_right / largest,
    )


def combine_moebius(earlier, later):
    return moebius_product(later, earlier)


def combine_affine(earlier, later):
    return (later[0] * earlier[0], later[1] + later[0][None, :] * earlier[1])


def pivot_step(inverse_matrix, inputs):
    current_diagonal, couple_now = inputs
    pivot = current_diagonal - couple_now * inverse_matrix
    return (1.0 / pivot, pivot)


def step_value_pair(carry, inputs):
    scaled_now, pivot, factor_now = inputs
    value = scaled_now + carry / pivot[None, :]
    return (factor_now[None, :] * value, value)


def local(spectrum, coupling, spatial_basis, noise_keys, noise_counters):
    steps_dev, modes = coupling.shape
    vec_count = noise_keys.shape[0]
    first_step = lax.axis_index("tm") * steps_dev
    first_mode = lax.axis_index("space") * modes
    ones = jnp.ones((modes,), jnp.float32)
    zeros = jnp.zeros((modes,), jnp.float32)
    step_ids = first_step + jnp.arange(steps_dev, dtype=jnp.int32)
    mode_ids = first_mode + jnp.arange(modes, dtype=jnp.int32)
    noise = noise_block(noise_keys, noise_counters, step_ids, mode_ids)
    diag_part = spectrum[None, :] * (1.0 + coupling * coupling)
    factor = spectrum[None, :] * coupling
    couple_square = factor * factor

    def fold_step(carry, inputs):
        current_diagonal, couple_now = inputs
        return (moebius_product((current_diagonal, -couple_now, ones, zeros), carry), None)

    local_map, _ = lax.scan(fold_step, (ones, zeros, zeros, ones), (diag_part, couple_square))
    incoming = entering(local_map, "tm", combine_moebius, (ones, zeros, zeros, ones), False)
    start_inverse = incoming[2] / incoming[0]
    _, pivots = lax.scan(pivot_step, start_inverse, (diag_part, couple_square))
    scaled = noise / jnp.sqrt(pivots)[:, None, :]

    def compose_step(carry, inputs):
        gain, offset = carry
        scaled_now, pivot, factor_now = inputs
        return (
            (
                factor_now * gain / pivot,
                factor_now[None, :] * (scaled_now + offset / pivot[None, :]),
            ),
            None,
        )

    empty_state = jnp.zeros((vec_count, modes), jnp.float32)
    local_affine, _ = lax.scan(
        compose_step, (ones, empty_state), (scaled, pivots, factor), reverse=True
    )
    _, carry_in = entering(local_affine, "tm", combine_affine, (ones, empty_state), True)
    _, mode_values = lax.scan(step_value_pair, carry_in, (scaled, pivots, factor), reverse=True)
    rounded = mode_values.astype(jnp.bfloat16)
    rows_here = spatial_basis.shape[0] // lax.axis_size("space")
    node_rows = lax.all_to_all(spatial_basis, "space", split_axis=0, concat_axis=1, tiled=True)
    image = jnp.einsum(
        "nk,tvk->ntv", node_rows, collect(rounded, "space", 2), preferred_element_type=jnp.float32
    )
    return image.reshape(jnp.zeros((rows_here, steps_dev * vec_count), jnp.float32).shape)


def solution(mesh):
    in_specs = (P("space"), P("tm", "space"), P(None, "space"), P(), P())
    out_specs = P("space", "tm")
    return jax.shard_map(local, mesh=mesh, in_specs=in_specs, out_specs=out_specs, check_vma=False)
```

profile of v0, /device:TPU:1, one launch (start us, length us, event | category | flops | bytes accessed | tf_op | source)
XLA Modules:
  0.0 149.9 jit_solution(11203134654924881383)
XLA Ops:
  0.0 0.7 fusion.38
  0.7 0.5 while.64
  1.2 0.6 broadcast_in_dim.102
  1.8 16.8 %all-to-all-start = ((f32[32,4,128]{2,1,0:T(4,128)}), f32[32,4,128]{2,1,0:T(4,128)S(1)}, u32[]{:S(2)}, u32[]{:S(2)}) async-start(f32[32,4,128]{2,1,0:T(4,128)} %broadcast_in_dim.102), calls=%async_computation | async-start | bytes 131072 | tf_op jit(solution)/shard_map/all_to_all | solution.py:9
  18.6 0.7 broadcast_multiply_fusion.2
  19.3 0.7 multiply_add_fusion.10
  20.0 11.6 %all-to-all-done = f32[32,4,128]{2,1,0:T(4,128)S(1)} async-done(((f32[32,4,128]{2,1,0:T(4,128)}), f32[32,4,128]{2,1,0:T(4,128)S(1)}, u32[]{:S(2)}, u32[]{:S(2)}) %all-to-all-start) | async-done | bytes 65568 | tf_op jit(solution)/shard_map/all_to_all | solution.py:9
  31.7 0.1 broadcast_select_fusion.6
  32.5 0.6 while.62
  33.1 1.2 fusion.25
  34.3 0.5 while.65
  34.8 1.1 broadcast_in_dim.106
  36.0 5.2 %all-to-all-start.1 = ((f32[32,65,128]{2,1,0:T(8,128)}), f32[32,65,128]{2,1,0:T(8,128)S(1)}, u32[]{:S(2)}, u32[]{:S(2)}) async-start(f32[32,65,128]{2,1,0:T(8,128)} %broadcast_in_dim.106), calls=%async_computation.1 | async-start | bytes 2359296 | tf_op jit(solution)/shard_map/all_to_all | solution.py:9
  41.2 61.3 %all-to-all-done.1 = f32[32,65,128]{2,1,0:T(8,128)S(1)} async-done(((f32[32,65,128]{2,1,0:T(8,128)}), f32[32,65,128]{2,1,0:T(8,128)S(1)}, u32[]{:S(2)}, u32[]{:S(2)}) %all-to-all-start.1) | async-done | bytes 1064992 | tf_op jit(solution)/shard_map/all_to_all | solution.py:9
  102.5 6.8 %all-to-all-start.3 = ((bf16[16,128,128]{2,1,0:T(8,128)(2,1)}), bf16[16,128,128]{2,1,0:T(8,128)(2,1)S(1)}, u32[]{:S(2)}, u32[]{:S(2)}) async-start(bf16[16,128,128]{2,1,0:T(8,128)(2,1)} %bitcast.21), calls=%async_computation.3 | async-start | bytes 1048576 | tf_op jit(solution)/shard_map/all_to_all | solution.py:169
  109.3 0.1 broadcast_select_fusion.5
  109.6 0.1 slice_select_fusion
  109.7 0.1 fusion.39
  109.8 0.1 multiply_add_fusion.2
  110.0 0.7 while.63
  110.7 7.6 %all-to-all-done.3 = bf16[16,128,128]{2,1,0:T(8,128)(2,1)S(1)} async-done(((bf16[16,128,128]{2,1,0:T(8,128)(2,1)}), bf16[16,128,128]{2,1,0:T(8,128)(2,1)S(1)}, u32[]{:S(2)}, u32[]{:S(2)}) %all-to-all-start.3) | async-done | bytes 524320 | tf_op jit(solution)/shard_map/all_to_all | solution.py:169
  118.3 0.5 broadcast_in_dim.110
  118.8 29.6 %all_to_all.31 = bf16[16,8,64,128]{3,2,1,0:T(8,128)(2,1)S(1)} all-to-all(bf16[16,8,64,128]{3,2,1,0:T(8,128)(2,1)S(1)} %broadcast_in_dim.110), channel_id=1, replica_groups=mesh['tm'=32,'space'=16] {'space'}, dimensions={0} | all-to-all | bytes 4194304 | tf_op jit(solution)/shard_map/all_to_all | solution.py:9
  148.4 0.7 fusion.12
  149.1 0.8 copy.16
  (149 shorter events, 2.4 us)
Async XLA Ops:
  1.8 29.8 %all-to-all-start = ((f32[32,4,128]{2,1,0:T(4,128)}), f32[32,4,128]{2,1,0:T(4,128)S(1)}, u32[]{:S(2)}, u32[]{:S(2)}) async-start(f32[32,4,128]{2,1,0:T(4,128)} %broadcast_in_dim.102), calls=%async_computation | async-start | bytes 131072 | tf_op jit(solution)/shard_map/all_to_all | solution.py:9
  36.0 66.5 %all-to-all-start.1 = ((f32[32,65,128]{2,1,0:T(8,128)}), f32[32,65,128]{2,1,0:T(8,128)S(1)}, u32[]{:S(2)}, u32[]{:S(2)}) async-start(f32[32,65,128]{2,1,0:T(8,128)} %broadcast_in_dim.106), calls=%async_computation.1 | async-start | bytes 2359296 | tf_op jit(solution)/shard_map/all_to_all | solution.py:9
  102.5 15.8 %all-to-all-start.3 = ((bf16[16,128,128]{2,1,0:T(8,128)(2,1)}), bf16[16,128,128]{2,1,0:T(8,128)(2,1)S(1)}, u32[]{:S(2)}, u32[]{:S(2)}) async-start(bf16[16,128,128]{2,1,0:T(8,128)(2,1)} %bitcast.21), calls=%async_computation.3 | async-start | bytes 1048576 | tf_op jit(solution)/shard_map/all_to_all | solution.py:169
where the time goes:
time: 152 us; the launch traced here: 150 us
  waiting for transfers between devices  80.5 us (53%)
  blocking collectives  29.6 us (19%)
  starting transfers between devices  28.7 us (19%)
  other arithmetic  5 us (3%)
  local copies, waits for them, and re-layouts  4.29 us (3%)
    all_to_all x2, waiting for transfers between devices, copy_for_each(): return lax.all_to_all(copies, axis, split_axis=0, concat_axis=0, tiled=True)  73 us
    all_to_all x1, blocking collectives, copy_for_each(): return lax.all_to_all(copies, axis, split_axis=0, concat_axis=0, tiled=True)  29.6 us
    all_to_all x2, starting transfers between devices, copy_for_each(): return lax.all_to_all(copies, axis, split_axis=0, concat_axis=0, tiled=True)  21.9 us
    all_to_all x1, waiting for transfers between devices, local(): lax.all_to_all(spatial_basis, 'space', split_axis=0, concat_axis=1, tiled...  7.56 us
    all_to_all x1, starting transfers between devices, local(): lax.all_to_all(spatial_basis, 'space', split_axis=0, concat_axis=1, tiled...  6.76 us
  transfers between devices with their start and end apart: 3, of which 3 were waited for; matrix products, arithmetic and copies ran while one was open for 2% of the time, Pallas kernels for 0%

commit v1 on v0

v1 whole, which is shorter than its diff:
```python
import functools

import jax
import jax.numpy as jnp
from jax import lax
from jax.experimental import pallas as pl
from jax.experimental.pallas import tpu as pltpu
from jax.sharding import PartitionSpec as P

MESH = pl.DeviceIdType.MESH
F32, BF16, I32 = jnp.float32, jnp.bfloat16, jnp.int32
KEY_STEP, TIME_STEP, MODE_STEP = 668265261, 374761393, -1640531535
SINE = (
    6.283185160088995,
    -41.3416550313122,
    81.60100406725992,
    -76.54978216547879,
    39.536705154320686,
)


def mix_bits(h):
    h = h ^ lax.shift_right_logical(h, I32(16))
    h = h * I32(-2048144789)
    h = h ^ lax.shift_right_logical(h, I32(13))
    h = h * I32(-1028477387)
    return h ^ lax.shift_right_logical(h, I32(16))


def noise_of(h):
    first = mix_bits(h)
    second = mix_bits(first + I32(1013904223))
    unit = (lax.shift_right_logical(first, I32(8)).astype(F32) + 0.5) * (1.0 / 16777216.0)
    square = -2.0 * jnp.log(unit)
    radius = square * lax.rsqrt(jnp.maximum(square, 1e-30))
    turn = jnp.abs(lax.shift_right_arithmetic(second, I32(8)).astype(F32) + 0.5)
    y = 0.25 - turn * (1.0 / 16777216.0)
    y2 = y * y
    p = jnp.float32(SINE[-1])
    for c in SINE[-2::-1]:
        p = p * y2 + jnp.float32(c)
    return radius * (p * y)


def shifted(x, by, fill):
    return jnp.concatenate([jnp.full((by, x.shape[1]), fill, F32), x[:-by]], axis=0)


def kernel(
    zt, ns, steps, vecs,
    keys_ref, counters_ref, spec_ref, coup_ref, basis_ref, out_ref,
    base, cz, cs, ps, rows, kin, mine, nz_group, nz_own, omega, last, coef_s, coef_a, vals,
    send, recv, local_sem,
):
    modes = coup_ref.shape[1]
    nodes = basis_ref.shape[0] // ns
    half = vecs // 2
    me_t, me_s = lax.axis_index("tm"), lax.axis_index("space")
    core = lax.rem(me_t, 2)
    chip = me_t // 2
    top = 2 * chip + 1

    barrier = pltpu.get_barrier_semaphore()

    @pl.loop(1, zt)
    def _(j):
        pl.semaphore_signal(
            barrier, inc=1, device_id=(lax.rem(me_t + j, zt), me_s), device_id_type=MESH
        )

    @pl.loop(1, ns)
    def _(j):
        other = lax.rem(me_s + j, ns)
        pl.semaphore_signal(barrier, inc=1, device_id=(me_t, other), device_id_type=MESH)
        pl.semaphore_signal(
            barrier, inc=1, device_id=(me_t + 1 - 2 * core, other), device_id_type=MESH
        )

    lanes = lax.broadcasted_iota(I32, (1, modes), 1) * I32(MODE_STEP)
    for v in range(vecs):
        seed = keys_ref[v] * I32(KEY_STEP) + counters_ref[v] * I32(TIME_STEP)
        base[pl.ds(v, 1), :] = lanes + seed

    first_mode = me_s * modes * I32(MODE_STEP)

    n_group = (zt - top) * (steps // 2)

    def group_noise(lo, hi):
        @pl.loop(lo, hi)
        def _(w):
            seg = zt - 1 - w // (steps // 2)
            i = 2 * lax.rem(w, steps // 2)
            offset = first_mode + (seg * steps + i) * I32(TIME_STEP)
            h = base[pl.ds(pl.multiple_of(core * half, half), half), :] + offset
            nz_group[seg, i] = noise_of(h)
            nz_group[seg, i + 1] = noise_of(h + I32(TIME_STEP))

    def own_noise(lo, hi):
        @pl.loop(lo, hi)
        def _(w):
            block = w // steps
            i = lax.rem(w, steps)
            offset = block * modes * I32(MODE_STEP) + (me_t * steps + i) * I32(TIME_STEP)
            nz_own[block, i] = noise_of(base[...] + offset)

    n_own = ns * steps
    early = jnp.maximum(0, zt // 4 - chip) * 12
    early_group = jnp.minimum(early, n_group)
    group_noise(0, early_group)

    pl.semaphore_wait(barrier, zt - 1 + 2 * (ns - 1))

    def all_copies(count, make):
        @pl.loop(1, count)
        def _(j):
            make(j).start()

    def wait_bytes(ref, sem):
        pltpu.make_async_copy(ref, ref, sem).wait()

    def tile(index):
        return pl.ds(pl.multiple_of(index * steps, steps), steps)

    cz[tile(me_t), :] = coup_ref[...]
    cs[tile(me_s), :] = coup_ref[...]

    def to_line(j):
        return pltpu.make_async_remote_copy(
            src_ref=coup_ref, dst_ref=cz.at[tile(me_t)], send_sem=send.at[0], recv_sem=recv.at[0],
            device_id=(lax.rem(me_t + j, zt), me_s), device_id_type=MESH,
        )

    all_copies(zt, to_line)

    def coupling_to_plane(j):
        return pltpu.make_async_remote_copy(
            src_ref=coup_ref, dst_ref=cs.at[tile(me_s)], send_sem=send.at[1], recv_sem=recv.at[1],
            device_id=(me_t, lax.rem(me_s + j, ns)), device_id_type=MESH,
        )

    all_copies(ns, coupling_to_plane)

    def basis_to_plane(j):
        other = lax.rem(me_s + j, ns)
        return pltpu.make_async_remote_copy(
            src_ref=basis_ref.at[pl.ds(pl.multiple_of(other * nodes, nodes), nodes), :],
            dst_ref=rows.at[me_s], send_sem=send.at[2], recv_sem=recv.at[2],
            device_id=(me_t, other), device_id_type=MESH,
        )

    all_copies(ns, basis_to_plane)
    own_rows = pltpu.make_async_copy(
        basis_ref.at[pl.ds(pl.multiple_of(me_s * nodes, nodes), nodes), :],
        rows.at[me_s],
        local_sem,
    )
    own_rows.start()

    group_noise(early_group, n_group)
    own_noise(0, n_own // 2)

    wait_bytes(cz.at[pl.ds(0, (zt - 1) * steps)], recv.at[0])
    inverse_spec = 1.0 / spec_ref[...]
    c = [cz[pl.ds(i, zt, stride=steps), :] for i in range(steps)]
    alpha, beta = [jnp.ones((zt, modes), F32)], [jnp.zeros((zt, modes), F32)]
    for i in range(steps + 1):
        beta.append(beta[i] + alpha[i])
        if i < steps:
            alpha.append(alpha[i] * (c[i] * c[i]))
    pa, pb = alpha[steps], beta[steps]
    by = 1
    while by < zt:
        pb = shifted(pb, by, 0.0) + shifted(pa, by, 1.0) * pb
        pa = shifted(pa, by, 1.0) * pa
        by *= 2
    pa, pb = shifted(pa, 1, 1.0), shifted(pb, 1, 0.0)
    sums = [pb + pa * beta[i + 1] for i in range(steps + 1)]
    inverse = [1.0 / sums[i + 1] for i in range(steps)]
    keep = [sums[i] * inverse[i] for i in range(steps)]
    gain, weight = jnp.ones((zt, modes), F32), []
    for i in range(steps):
        inner = keep[i] * inverse_spec
        weight.append(gain * c[i] * (inner * lax.rsqrt(inner)))
        gain = gain * (c[i] * keep[i])
    segs = lax.broadcasted_iota(I32, (zt, modes), 0)
    reach = jnp.where(segs > top, gain, 1.0)
    by = 1
    while by < zt:
        reach = shifted(reach, by, 1.0) * reach
        by *= 2
    reach = shifted(reach, 1, 1.0)
    for i in range(steps):
        omega[i] = weight[i] * reach
    last[0] = keep[steps - 1]
    last[1] = gain
    last[2] = pa
    last[3] = pb

    mine[0:1, :] = last[2, pl.ds(me_t, 1), :]
    mine[1:2, :] = last[3, pl.ds(me_t, 1), :]
    mine[2:steps, :] = jnp.broadcast_to(inverse_spec, (steps - 2, modes))
    ps[tile(me_s), :] = mine[...]

    def start_to_plane(j):
        return pltpu.make_async_remote_copy(
            src_ref=mine, dst_ref=ps.at[tile(me_s)], send_sem=send.at[3], recv_sem=recv.at[3],
            device_id=(me_t, lax.rem(me_s + j, ns)), device_id_type=MESH,
        )

    all_copies(ns, start_to_plane)

    def summed(seg, carry):
        terms = [omega[i, pl.ds(seg, 1), :] * nz_group[seg, i] for i in range(steps)]
        while len(terms) > 1:
            terms = [terms[k] + terms[k + 1] for k in range(0, len(terms), 2)]
        return carry + terms[0]

    zero = jnp.zeros((half, modes), F32)
    carry_top = lax.fori_loop(top + 1, zt, summed, zero)
    carry_low = summed(top, last[1, pl.ds(top, 1), :] * carry_top)
    kin_top = (last[0, pl.ds(top, 1), :] * carry_top).astype(BF16)
    kin_low = (last[0, pl.ds(top - 1, 1), :] * carry_low).astype(BF16)
    slot = 2 * me_s + core

    out_low, out_top = kin.at[2 * ns], kin.at[2 * ns + 1]
    out_low[...] = kin_low
    out_top[...] = kin_top

    def low_to_plane(j):
        return pltpu.make_async_remote_copy(
            src_ref=out_low, dst_ref=kin.at[slot], send_sem=send.at[4], recv_sem=recv.at[4],
            device_id=(2 * chip, lax.rem(me_s + j, ns)), device_id_type=MESH,
        )

    def top_to_plane(j):
        return pltpu.make_async_remote_copy(
            src_ref=out_top, dst_ref=kin.at[slot], send_sem=send.at[4], recv_sem=recv.at[4],
            device_id=(top, lax.rem(me_s + j, ns)), device_id_type=MESH,
        )

    all_copies(ns, low_to_plane)
    all_copies(ns, top_to_plane)

    @pl.when(core == 0)
    def _():
        top_to_plane(0).start()
        kin[slot] = kin_low

    @pl.when(core == 1)
    def _():
        low_to_plane(0).start()
        kin[slot] = kin_top

    own_noise(n_own // 2, n_own)

    wait_bytes(cs.at[pl.ds(0, (ns - 1) * steps)], recv.at[1])
    wait_bytes(ps.at[pl.ds(0, (ns - 1) * steps)], recv.at[3])
    c = [cs[pl.ds(i, ns, stride=steps), :] for i in range(steps)]
    pa, pb, inv_s = [ps[pl.ds(i, ns, stride=steps), :] for i in range(3)]
    now = pb + pa
    for i in range(steps):
        pa = pa * (c[i] * c[i])
        after = now + pa
        kept = now / after
        inner = kept * inv_s
        coef_s[i] = inner * lax.rsqrt(inner)
        if i < steps - 1:
            coef_a[i] = kept * c[i + 1]
        now = after

    wait_bytes(rows.at[pl.ds(0, ns - 1)], recv.at[2])
    own_rows.wait()
    wait_bytes(kin.at[pl.ds(0, 2 * ns - 1)], recv.at[4])

    def block_of(b):
        value = jnp.concatenate([kin[2 * b], kin[2 * b + 1]], axis=0).astype(F32)
        for i in range(steps - 1, -1, -1):
            if i < steps - 1:
                value = coef_a[i, pl.ds(b, 1), :] * value
            value = value + coef_s[i, pl.ds(b, 1), :] * nz_own[b, i]
            vals[b, pl.ds(i * vecs, vecs), :] = value.astype(BF16)

    @pl.loop(0, ns)
    def _(b):
        block_of(b)

    def product(b):
        return lax.dot_general(
            rows[b], vals[b], (((1,), (1,)), ((), ())), preferred_element_type=F32
        )

    out_ref[...] = product(0)

    @pl.loop(1, ns)
    def _(b):
        out_ref[...] += product(b)

    wait_bytes(cz.at[pl.ds(0, (zt - 1) * steps)], send.at[0])
    wait_bytes(cs.at[pl.ds(0, (ns - 1) * steps)], send.at[1])
    wait_bytes(rows.at[pl.ds(0, ns - 1)], send.at[2])
    wait_bytes(ps.at[pl.ds(0, (ns - 1) * steps)], send.at[3])
    wait_bytes(kin.at[pl.ds(0, 2 * ns - 1)], send.at[4])


def solution(mesh):
    zt, ns = mesh.shape["tm"], mesh.shape["space"]

    def local(spectrum, coupling, spatial_basis, noise_keys, noise_counters):
        steps, modes = coupling.shape
        vecs = noise_keys.shape[0]
        nodes = spatial_basis.shape[0] // ns
        vmem, smem = pltpu.VMEM, pltpu.SMEM
        return pl.pallas_call(
            functools.partial(kernel, zt, ns, steps, vecs),
            out_shape=jax.ShapeDtypeStruct((nodes, steps * vecs), F32),
            in_specs=[
                pl.BlockSpec(memory_space=smem),
                pl.BlockSpec(memory_space=smem),
                pl.BlockSpec(memory_space=vmem),
                pl.BlockSpec(memory_space=vmem),
                pl.BlockSpec(memory_space=pl.ANY),
            ],
            out_specs=pl.BlockSpec(memory_space=vmem),
            scratch_shapes=[
                vmem((vecs, modes), I32),
                vmem((zt * steps, modes), F32),
                vmem((ns * steps, modes), F32),
                vmem((ns * steps, modes), F32),
                vmem((ns, nodes, modes), BF16),
                vmem((2 * ns + 2, vecs // 2, modes), BF16),
                vmem((steps, modes), F32),
                vmem((zt, steps, vecs // 2, modes), F32),
                vmem((ns, steps, vecs, modes), F32),
                vmem((steps, zt, modes), F32),
                vmem((4, zt, modes), F32),
                vmem((steps, ns, modes), F32),
                vmem((steps, ns, modes), F32),
                vmem((ns, steps * vecs, modes), BF16),
                pltpu.SemaphoreType.DMA((5,)),
                pltpu.SemaphoreType.DMA((5,)),
                pltpu.SemaphoreType.DMA,
            ],
            compiler_params=pltpu.CompilerParams(
                collective_id=0, has_side_effects=True, vmem_limit_bytes=48 * 2**20
            ),
        )(noise_keys, noise_counters, spectrum.reshape(1, modes), coupling, spatial_basis)

    return jax.shard_map(
        local,
        mesh=mesh,
        in_specs=(P("space"), P("tm", "space"), P(None, "space"), P(), P()),
        out_specs=P("space", "tm"),
        check_vma=False,
    )
```

time: 152 us -> 41.4 us (0.27); the launches traced: 150 us -> 41.2 us
  waiting for transfers between devices: 80.5 us -> 0 us
  Pallas kernels: 0 us -> 38.1 us
  blocking collectives: 29.6 us -> 0 us
  starting transfers between devices: 28.7 us -> 0 us
  other arithmetic: 5 us -> 0 us
    all_to_all x3 -> x0, waiting for transfers between devices: 80.5 us -> none  [the longest x2 73 us: copy_for_each(): return lax.all_to_all(copies, axis, split_axis=0, concat_axis=0, tiled=True)]
    pallas_call x0 -> x1, Pallas kernels: none -> 38.1 us  [local(): pl.pallas_call(functools.partial(kernel, zt, ns, steps, vecs), out_shape=...]
    all_to_all x1 -> x0, blocking collectives: 29.6 us -> none  [copy_for_each(): return lax.all_to_all(copies, axis, split_axis=0, concat_axis=0, tiled=True)]
    all_to_all x3 -> x0, starting transfers between devices: 28.7 us -> none  [the longest x2 21.9 us: copy_for_each(): return lax.all_to_all(copies, axis, split_axis=0, concat_axis=0, tiled=True)]
    unnamed x0 -> x11, local copies, waits for them, and re-layouts: none -> 3.11 us
    broadcast_in_dim x4 -> x0, local copies, waits for them, and re-layouts: 2.3 us -> none  [the longest x3 2.28 us: copy_for_each(): copies = jnp.broadcast_to(x, (lax.axis_size(axis), *x.shape))]
    div x42 -> x0, other arithmetic: 1.96 us -> none  [the longest x1 1.24 us: local(): scaled = noise / jnp.sqrt(pivots)[:, None, :]]
    mul x23 -> x0, other arithmetic: 1.65 us -> none  [the longest x1 0.69 us: local(): couple_square = factor * factor]
  transfers between devices with their start and end apart: 3 -> 0, of which waited for: 3 -> 0; matrix products, arithmetic and copies ran while one was open for 2% -> 0% of each run, Pallas kernels for 0% -> 0%
where the time goes in v1:
time: 41.4 us; the launch traced here: 41.2 us
  Pallas kernels  38.1 us (92%)
  local copies, waits for them, and re-layouts  3.11 us (8%)
    pallas_call x1, Pallas kernels, local(): pl.pallas_call(functools.partial(kernel, zt, ns, steps, vecs), out_shape=...  38.1 us
    unnamed x11, local copies, waits for them, and re-layouts  3.11 us

profile of v1, /device:TPU:1, one launch (start us, length us, event | category | flops | bytes accessed | tf_op | source)
XLA Modules:
  0.0 41.2 jit_solution(14284874375834938304)
XLA Ops:
  0.0 0.0 copy-start.3
  0.0 0.0 copy-start.2
  0.0 0.0 copy-start.4
  0.0 0.6 %copy-done.3 = s32[64]{0:T(128)S(1)} copy-done((s32[64]{0:T(128)S(1)}, s32[64]{0:T(128)}, u32[]{:S(2)}) %copy-start.3) | copy-done | bytes 280
  0.7 0.0 copy-done.2
  0.7 0.0 copy-done.4
  0.7 0.0 copy-start
  0.7 1.0 %copy-done = bf16[2048,128]{1,0:T(8,128)(2,1)S(1)} copy-done((bf16[2048,128]{1,0:T(8,128)(2,1)S(1)}, bf16[2048,128]{1,0:T(8,128)(2,1)}, u32[]{:S(2)}) %copy-start) | copy-done | bytes 524312
  1.7 0.0 copy-start.1
  1.7 0.7 %copy-done.1 = f32[8,128]{1,0:T(8,128)S(1)} copy-done((f32[8,128]{1,0:T(8,128)S(1)}, f32[8,128]{1,0:T(8,128)}, u32[]{:S(2)}) %copy-start.1) | copy-done | bytes 4120
  2.4 38.1 %shard_map.55 = f32[128,512]{1,0:T(8,128)S(1)} custom-call(s32[64]{0:T(128)S(1)} %copy-done.2, s32[64]{0:T(128)S(1)} %copy-done.3, f32[1,128]{1,0:T(1,128)S(1)} %bitcast.1, f32[8,128]{1,0:T(8,128)S(1)} %copy-done.1, bf16[2048,128]{1,0:T(8,128)(2,1)S(1)} %copy-done), custom_call_target="tpu_custom_call" | custom-call | tf_op jit(solution)/shard_map/pallas_call | solution.py:313
  40.5 0.7 %copy.7 = f32[128,512]{1,0:T(8,128)} copy(f32[128,512]{1,0:T(8,128)S(1)} %shard_map.55) | data formatting | bytes 524288
Async XLA Ops:
  0.0 0.7 %copy-start.3 = (s32[64]{0:T(128)S(1)}, s32[64]{0:T(128)}, u32[]{:S(2)}) copy-start(s32[64]{0:T(128)} %counters_ref.1) | copy-start | bytes 772
  0.0 0.7 %copy-start.2 = (s32[64]{0:T(128)S(1)}, s32[64]{0:T(128)}, u32[]{:S(2)}) copy-start(s32[64]{0:T(128)} %keys_ref.1) | copy-start | bytes 772
  0.0 0.7 %copy-start.4 = (f32[128]{0:T(128)S(1)}, f32[128]{0:T(128)}, u32[]{:S(2)}) copy-start(f32[128]{0:T(128)} %param.5) | copy-start | bytes 1540
  0.7 1.0 %copy-start = (bf16[2048,128]{1,0:T(8,128)(2,1)S(1)}, bf16[2048,128]{1,0:T(8,128)(2,1)}, u32[]{:S(2)}) copy-start(bf16[2048,128]{1,0:T(8,128)(2,1)} %basis_ref.1) | copy-start | bytes 1572868
  1.7 0.7 %copy-start.1 = (f32[8,128]{1,0:T(8,128)S(1)}, f32[8,128]{1,0:T(8,128)}, u32[]{:S(2)}) copy-start(f32[8,128]{1,0:T(8,128)} %coup_ref.1) | copy-start | bytes 12292

commit v2 on v1

v2 whole, which is shorter than its diff:
```python
import functools

import jax
import jax.numpy as jnp
from jax import lax
from jax.experimental import pallas as pl
from jax.experimental.pallas import tpu as pltpu
from jax.sharding import PartitionSpec as P

MESH = pl.DeviceIdType.MESH
F32, BF16, I32 = jnp.float32, jnp.bfloat16, jnp.int32
KEY_STEP, TIME_STEP, MODE_STEP = 668265261, 374761393, -1640531535
SINE = (
    6.283185160088995,
    -41.3416550313122,
    81.60100406725992,
    -76.54978216547879,
    39.536705154320686,
)


def mix_bits(h):
    h = h ^ lax.shift_right_logical(h, I32(16))
    h = h * I32(-2048144789)
    h = h ^ lax.shift_right_logical(h, I32(13))
    h = h * I32(-1028477387)
    return h ^ lax.shift_right_logical(h, I32(16))


def noise_of(h):
    first = mix_bits(h)
    second = mix_bits(first + I32(1013904223))
    unit = (lax.shift_right_logical(first, I32(8)).astype(F32) + 0.5) * (1.0 / 16777216.0)
    square = -2.0 * jnp.log(unit)
    radius = square * lax.rsqrt(jnp.maximum(square, 1e-30))
    turn = jnp.abs(lax.shift_right_arithmetic(second, I32(8)).astype(F32) + 0.5)
    y = 0.25 - turn * (1.0 / 16777216.0)
    y2 = y * y
    p = jnp.float32(SINE[-1])
    for c in SINE[-2::-1]:
        p = p * y2 + jnp.float32(c)
    return radius * (p * y)


def shifted(x, by, fill):
    return jnp.concatenate([jnp.full((by, x.shape[1]), fill, F32), x[:-by]], axis=0)


def kernel(
    zt, ns, steps, vecs,
    keys_hbm, counters_hbm, spec_hbm, coup_hbm, basis_ref, out_ref,
    keys_ref, counters_ref, spec_ref, coup_ref, base, cz, cs, ps, rows, kin, mine,
    nz_group, nz_own, omega, above, coef_s, coef_a, vals,
    send, recv, local_sem,
):
    modes = coup_ref.shape[1]
    nodes = basis_ref.shape[0] // ns
    half = vecs // 2
    chips, long = zt // 2, 2 * steps
    me_t, me_s = lax.axis_index("tm"), lax.axis_index("space")
    core = lax.rem(me_t, 2)
    sibling = me_t + 1 - 2 * core
    chip = me_t // 2

    barrier = pltpu.get_barrier_semaphore()

    def greet(t, s):
        pl.semaphore_signal(barrier, inc=1, device_id=(t, s), device_id_type=MESH)

    @pl.loop(1, chips)
    def _(j):
        greet(lax.rem(me_t + 2 * j, zt), me_s)

    greet(sibling, me_s)

    @pl.loop(1, ns)
    def _(j):
        other = lax.rem(me_s + j, ns)
        greet(me_t, other)
        greet(sibling, other)

    loads = [
        pltpu.make_async_copy(src, dst, local_sem.at[k])
        for k, (src, dst) in enumerate(
            [
                (keys_hbm, keys_ref),
                (counters_hbm, counters_ref),
                (spec_hbm, spec_ref),
                (coup_hbm, coup_ref),
                (
                    basis_ref.at[pl.ds(pl.multiple_of(me_s * nodes, nodes), nodes), :],
                    rows.at[me_s],
                ),
            ]
        )
    ]
    for load in loads:
        load.start()
    loads[0].wait()
    loads[1].wait()

    lanes = lax.broadcasted_iota(I32, (1, modes), 1) * I32(MODE_STEP)
    for v in range(vecs):
        seed = keys_ref[v] * I32(KEY_STEP) + counters_ref[v] * I32(TIME_STEP)
        base[pl.ds(v, 1), :] = lanes + seed

    first_mode = me_s * modes * I32(MODE_STEP)

    n_group = (chips - 1 - chip) * steps + steps // 2

    def group_noise(lo, hi):
        @pl.loop(lo, hi)
        def _(w):
            there = chips - 1 - w // steps
            i = 2 * (steps - 1 - lax.rem(w, steps))
            offset = first_mode + (there * long + i) * I32(TIME_STEP)
            h = base[pl.ds(pl.multiple_of(core * half, half), half), :] + offset
            nz_group[there, i] = noise_of(h)
            nz_group[there, i + 1] = noise_of(h + I32(TIME_STEP))

    def own_noise(lo, hi):
        @pl.loop(lo, hi)
        def _(w):
            block = w // steps
            i = lax.rem(w, steps)
            offset = block * modes * I32(MODE_STEP) + (me_t * steps + i) * I32(TIME_STEP)
            nz_own[block, i] = noise_of(base[...] + offset)

    n_own = ns * steps
    early = jnp.where(chip < chips // 2, 200 - 17 * chip, 20)
    late = jnp.where(chip < chips // 2, 0, n_own // 4)
    early_group = jnp.minimum(early, n_group)
    early_own = jnp.minimum(early - early_group, n_own)
    group_noise(0, early_group)
    own_noise(0, early_own)

    def wait_bytes(ref, sem):
        pltpu.make_async_copy(ref, ref, sem).wait()

    def tile(index):
        return pl.ds(pl.multiple_of(index * steps, steps), steps)

    loads[3].wait()
    mine_at = core * chips + chip
    cz[tile(mine_at), :] = coup_ref[...]
    cs[tile(me_s), :] = coup_ref[...]
    pl.semaphore_wait(barrier, chips - 1 + 1 + 2 * (ns - 1))

    @pl.loop(0, chips - 1)
    def _(j):
        to = j + (j >= chip).astype(I32)
        pltpu.make_async_remote_copy(
            src_ref=coup_ref, dst_ref=cz.at[tile(mine_at)], send_sem=send.at[0], recv_sem=recv.at[0],
            device_id=(2 * to + core, me_s), device_id_type=MESH,
        ).start()

    def all_copies(make):
        @pl.loop(1, ns)
        def _(j):
            make(lax.rem(me_s + j, ns)).start()

    def coupling_to_plane(other):
        return pltpu.make_async_remote_copy(
            src_ref=coup_ref, dst_ref=cs.at[tile(me_s)], send_sem=send.at[1], recv_sem=recv.at[1],
            device_id=(me_t, other), device_id_type=MESH,
        )

    all_copies(coupling_to_plane)

    def basis_to_plane(other):
        return pltpu.make_async_remote_copy(
            src_ref=basis_ref.at[pl.ds(pl.multiple_of(other * nodes, nodes), nodes), :],
            dst_ref=rows.at[me_s], send_sem=send.at[2], recv_sem=recv.at[2],
            device_id=(me_t, other), device_id_type=MESH,
        )

    all_copies(basis_to_plane)

    group_noise(early_group, n_group)
    own_noise(early_own, jnp.maximum(early_own, n_own - late))

    wait_bytes(cz.at[pl.ds(0, (chips - 1) * steps)], recv.at[0])
    line = pl.ds(pl.multiple_of(core * chips * steps, steps), chips * steps)
    across = pltpu.make_async_remote_copy(
        src_ref=cz.at[line], dst_ref=cz.at[line], send_sem=send.at[5], recv_sem=recv.at[5],
        device_id=(sibling, me_s), device_id_type=MESH,
    )
    across.start()
    loads[2].wait()
    inverse_spec = 1.0 / spec_ref[...]
    across.wait_recv()

    c = [
        cz[pl.ds(p * chips * steps + i, chips, stride=steps), :]
        for p in range(2)
        for i in range(steps)
    ]
    one, nil = jnp.ones((chips, modes), F32), jnp.zeros((chips, modes), F32)
    alpha, beta = [one], [nil]
    for i in range(long + 1):
        beta.append(beta[i] + alpha[i])
        if i < long:
            alpha.append(alpha[i] * (c[i] * c[i]))
    pa, pb = alpha[long], beta[long]
    by = 1
    while by < chips:
        pb = shifted(pb, by, 0.0) + shifted(pa, by, 1.0) * pb
        pa = shifted(pa, by, 1.0) * pa
        by *= 2
    pa, pb = shifted(pa, 1, 1.0), shifted(pb, 1, 0.0)

    above[0] = jnp.where(core == 0, pa, pa * alpha[steps])
    above[1] = jnp.where(core == 0, pb, pb + pa * beta[steps])
    mine[0:1, :] = above[0, pl.ds(chip, 1), :]
    mine[1:2, :] = above[1, pl.ds(chip, 1), :]
    mine[2:steps, :] = jnp.broadcast_to(inverse_spec, (steps - 2, modes))
    ps[tile(me_s), :] = mine[...]

    def start_to_plane(other):
        return pltpu.make_async_remote_copy(
            src_ref=mine, dst_ref=ps.at[tile(me_s)], send_sem=send.at[3], recv_sem=recv.at[3],
            device_id=(me_t, other), device_id_type=MESH,
        )

    all_copies(start_to_plane)

    sums = [pb + pa * beta[i + 1] for i in range(long + 1)]
    inverse = [1.0 / sums[i + 1] for i in range(long)]
    keep = [sums[i] * inverse[i] for i in range(long)]
    gains, weight = [], []
    for first in (0, steps):
        gain = one
        for i in range(first, first + steps):
            inner = keep[i] * inverse_spec
            weight.append(gain * c[i] * (inner * lax.rsqrt(inner)))
            gain = gain * (c[i] * keep[i])
        gains.append(gain)
    numbers = lax.broadcasted_iota(I32, (chips, modes), 0)
    reach = jnp.where(numbers > chip, gains[0] * gains[1], 1.0)
    by = 1
    while by < chips:
        reach = shifted(reach, by, 1.0) * reach
        by *= 2
    reach = shifted(reach, 1, 1.0)
    middle = reach * gains[0]
    for i in range(steps):
        omega[i] = weight[i] * reach
        omega[steps + i] = weight[steps + i] * middle
        above[5 + i] = weight[steps + i]
    above[2] = keep[long - 1]
    above[3] = keep[steps - 1]
    above[4] = gains[1]

    def added(terms):
        while len(terms) > 1:
            terms = [terms[k] + terms[k + 1] for k in range(0, len(terms), 2)]
        return terms[0]

    def summed(there, carry):
        return carry + added(
            [omega[i, pl.ds(there, 1), :] * nz_group[there, i] for i in range(long)]
        )

    carry_top = lax.fori_loop(chip + 1, chips, summed, jnp.zeros((half, modes), F32))
    carry_low = above[4, pl.ds(chip, 1), :] * carry_top + added(
        [above[5 + i, pl.ds(chip, 1), :] * nz_group[chip, steps + i] for i in range(steps)]
    )
    kin_top = (above[2, pl.ds(chip, 1), :] * carry_top).astype(BF16)
    kin_low = (above[3, pl.ds(chip, 1), :] * carry_low).astype(BF16)
    slot = 2 * me_s + core

    out_low, out_top = kin.at[2 * ns], kin.at[2 * ns + 1]
    out_low[...] = kin_low
    out_top[...] = kin_top

    def low_to_plane(other):
        return pltpu.make_async_remote_copy(
            src_ref=out_low, dst_ref=kin.at[slot], send_sem=send.at[4], recv_sem=recv.at[4],
            device_id=(2 * chip, other), device_id_type=MESH,
        )

    def top_to_plane(other):
        return pltpu.make_async_remote_copy(
            src_ref=out_top, dst_ref=kin.at[slot], send_sem=send.at[4], recv_sem=recv.at[4],
            device_id=(2 * chip + 1, other), device_id_type=MESH,
        )

    all_copies(low_to_plane)
    all_copies(top_to_plane)

    @pl.when(core == 0)
    def _():
        top_to_plane(me_s).start()
        kin[slot] = kin_low

    @pl.when(core == 1)
    def _():
        low_to_plane(me_s).start()
        kin[slot] = kin_top

    own_noise(jnp.maximum(early_own, n_own - late), n_own)

    wait_bytes(cs.at[pl.ds(0, (ns - 1) * steps)], recv.at[1])
    wait_bytes(ps.at[pl.ds(0, (ns - 1) * steps)], recv.at[3])
    c = [cs[pl.ds(i, ns, stride=steps), :] for i in range(steps)]
    pa, pb, inv_s = [ps[pl.ds(i, ns, stride=steps), :] for i in range(3)]
    now = pb + pa
    for i in range(steps):
        pa = pa * (c[i] * c[i])
        after = now + pa
        kept = now / after
        inner = kept * inv_s
        coef_s[i] = inner * lax.rsqrt(inner)
        if i < steps - 1:
            coef_a[i] = kept * c[i + 1]
        now = after

    wait_bytes(rows.at[pl.ds(0, ns - 1)], recv.at[2])
    loads[4].wait()
    wait_bytes(kin.at[pl.ds(0, 2 * ns - 1)], recv.at[4])

    for b in range(ns):
        value = jnp.concatenate([kin[2 * b], kin[2 * b + 1]], axis=0).astype(F32)
        for i in range(steps - 1, -1, -1):
            if i < steps - 1:
                value = coef_a[i, pl.ds(b, 1), :] * value
            value = value + coef_s[i, pl.ds(b, 1), :] * nz_own[b, i]
            vals[b, pl.ds(i * vecs, vecs), :] = value.astype(BF16)
        product = lax.dot_general(
            rows[b], vals[b], (((1,), (1,)), ((), ())), preferred_element_type=F32
        )
        if b == 0:
            out_ref[...] = product
        else:
            out_ref[...] += product

    wait_bytes(cz.at[pl.ds(0, (chips - 1) * steps)], send.at[0])
    wait_bytes(cs.at[pl.ds(0, (ns - 1) * steps)], send.at[1])
    wait_bytes(rows.at[pl.ds(0, ns - 1)], send.at[2])
    wait_bytes(ps.at[pl.ds(0, (ns - 1) * steps)], send.at[3])
    wait_bytes(kin.at[pl.ds(0, 2 * ns - 1)], send.at[4])
    across.wait_send()


def solution(mesh):
    zt, ns = mesh.shape["tm"], mesh.shape["space"]

    def local(spectrum, coupling, spatial_basis, noise_keys, noise_counters):
        steps, modes = coupling.shape
        vecs = noise_keys.shape[0]
        nodes = spatial_basis.shape[0] // ns
        vmem, smem = pltpu.VMEM, pltpu.SMEM
        return pl.pallas_call(
            functools.partial(kernel, zt, ns, steps, vecs),
            out_shape=jax.ShapeDtypeStruct((nodes, steps * vecs), F32),
            in_specs=[pl.BlockSpec(memory_space=pltpu.HBM)] * 5,
            out_specs=pl.BlockSpec(memory_space=vmem),
            scratch_shapes=[
                smem((vecs,), I32),
                smem((vecs,), I32),
                vmem((1, modes), F32),
                vmem((steps, modes), F32),
                vmem((vecs, modes), I32),
                vmem((zt * steps, modes), F32),
                vmem((ns * steps, modes), F32),
                vmem((ns * steps, modes), F32),
                vmem((ns, nodes, modes), BF16),
                vmem((2 * ns + 2, vecs // 2, modes), BF16),
                vmem((steps, modes), F32),
                vmem((zt // 2, 2 * steps, vecs // 2, modes), F32),
                vmem((ns, steps, vecs, modes), F32),
                vmem((2 * steps, zt // 2, modes), F32),
                vmem((5 + steps, zt // 2, modes), F32),
                vmem((steps, ns, modes), F32),
                vmem((steps, ns, modes), F32),
                vmem((ns, steps * vecs, modes), BF16),
                pltpu.SemaphoreType.DMA((6,)),
                pltpu.SemaphoreType.DMA((6,)),
                pltpu.SemaphoreType.DMA((5,)),
            ],
            compiler_params=pltpu.CompilerParams(
                collective_id=0, has_side_effects=True, vmem_limit_bytes=62 * 2**20
            ),
        )(noise_keys, noise_counters, spectrum.reshape(1, modes), coupling, spatial_basis)

    return jax.shard_map(
        local,
        mesh=mesh,
        in_specs=(P("space"), P("tm", "space"), P(None, "space"), P(), P()),
        out_specs=P("space", "tm"),
        check_vma=False,
    )
```

time: 41.4 us -> 37.3 us (0.901)
  Pallas kernels: 38.1 us -> 35.4 us
  local copies, waits for them, and re-layouts: 3.11 us -> 1.67 us
    pallas_call x1, Pallas kernels: 38.1 us -> 35.4 us  [local(): pl.pallas_call(functools.partial(kernel, zt, ns, steps, vecs), out_shape=...]
    unnamed x11 -> x1, local copies, waits for them, and re-layouts: 3.11 us -> 1.67 us
where the time goes in v2:
time: 37.3 us; the launch traced here: 37.1 us
  Pallas kernels  35.4 us (95%)
  local copies, waits for them, and re-layouts  1.67 us (4%)
    pallas_call x1, Pallas kernels, local(): pl.pallas_call(functools.partial(kernel, zt, ns, steps, vecs), out_shape=...  35.4 us
    unnamed x1, local copies, waits for them, and re-layouts  1.67 us

profile of v2, /device:TPU:1, one launch (start us, length us, event | category | flops | bytes accessed | tf_op | source)
XLA Modules:
  0.0 37.1 jit_solution(3171496228474031753)
XLA Ops:
  0.0 35.4 %shard_map.55 = f32[128,512]{1,0:T(8,128)} custom-call(s32[64]{0:T(128)} %keys_hbm.1, s32[64]{0:T(128)} %counters_hbm.1, f32[1,128]{1,0:T(1,128)} %bitcast.1, f32[8,128]{1,0:T(8,128)} %coup_hbm.1, bf16[2048,128]{1,0:T(8,128)(2,1)} %basis_ref.1), custom_call_target="tpu_custom_call" | custom-call | tf_op jit(solution)/shard_map/pallas_call | solution.py:353
  35.4 1.7 %copy.7 = f32[128,512]{1,0:T(8,128)} copy(f32[128,512]{1,0:T(8,128)} %shard_map.55) | data formatting | bytes 524288

commit v3 on v2

--- a/solution.py
+++ b/solution.py
@@ -49,9 +49,9 @@
 def kernel(
     zt, ns, steps, vecs,
     keys_hbm, counters_hbm, spec_hbm, coup_hbm, basis_ref, out_ref,
-    keys_ref, counters_ref, spec_ref, coup_ref, base, cz, cs, ps, rows, kin, mine,
-    nz_group, nz_own, omega, above, coef_s, coef_a, vals,
-    send, recv, local_sem,
+    keys_ref, counters_ref, spec_ref, coup_ref, base, fixed, cz, cs, ps, rows, kin, mine,
+    nz, omega, above, coef_s, coef_a, vals,
+    send, recv, local_sem, meet,
 ):
     modes = coup_ref.shape[1]
     nodes = basis_ref.shape[0] // ns
@@ -62,22 +62,38 @@
     sibling = me_t + 1 - 2 * core
     chip = me_t // 2
 
+    split, outer = chips // 2, chips * 3 // 4
+    leading = chip < split
+    inner = jnp.logical_and(chip >= split, chip < outer)
+    is_hub = chip == split - 1
+    line_in, near_in, plane_in, line_go, plane_go = (meet.at[k] for k in range(5))
     barrier = pltpu.get_barrier_semaphore()
 
-    def greet(t, s):
-        pl.semaphore_signal(barrier, inc=1, device_id=(t, s), device_id_type=MESH)
-
-    @pl.loop(1, chips)
-    def _(j):
-        greet(lax.rem(me_t + 2 * j, zt), me_s)
-
-    greet(sibling, me_s)
-
-    @pl.loop(1, ns)
-    def _(j):
-        other = lax.rem(me_s + j, ns)
-        greet(me_t, other)
-        greet(sibling, other)
+    def signal(sem, t, s):
+        pl.semaphore_signal(sem, inc=1, device_id=(t, s), device_id_type=MESH)
+
+    def signal_plane(sem):
+        signal(sem, sibling, me_s)
+
+        @pl.loop(1, ns)
+        def _(j):
+            other = lax.rem(me_s + j, ns)
+            signal(sem, me_t, other)
+            signal(sem, sibling, other)
+
+    @pl.when(leading)
+    def _():
+        @pl.loop(1, chips)
+        def _(j):
+            signal(barrier, lax.rem(me_t + 2 * j, zt), me_s)
+
+    @pl.when(jnp.logical_not(inner))
+    def _():
+        signal_plane(barrier)
+
+    def half_rows(owner):
+        start = owner * nodes + core * (nodes // 2)
+        return pl.ds(pl.multiple_of(start, nodes // 2), nodes // 2)
 
     loads = [
         pltpu.make_async_copy(src, dst, local_sem.at[k])
@@ -87,10 +103,7 @@
                 (counters_hbm, counters_ref),
                 (spec_hbm, spec_ref),
                 (coup_hbm, coup_ref),
-                (
-                    basis_ref.at[pl.ds(pl.multiple_of(me_s * nodes, nodes), nodes), :],
-                    rows.at[me_s],
-                ),
+                (basis_ref.at[half_rows(me_s), :], rows.at[core, me_s]),
             ]
         )
     ]
@@ -102,37 +115,39 @@
     lanes = lax.broadcasted_iota(I32, (1, modes), 1) * I32(MODE_STEP)
     for v in range(vecs):
         seed = keys_ref[v] * I32(KEY_STEP) + counters_ref[v] * I32(TIME_STEP)
-        base[pl.ds(v, 1), :] = lanes + seed
-
-    first_mode = me_s * modes * I32(MODE_STEP)
-
-    n_group = (chips - 1 - chip) * steps + steps // 2
-
-    def group_noise(lo, hi):
+        base[0, pl.ds(v, 1), :] = lanes + seed
+
+    halved = base[0, pl.ds(pl.multiple_of(core * half, half), half), :]
+    base[1, 0:half, :] = halved
+    base[1, half:vecs, :] = halved + I32(TIME_STEP)
+
+    n_group = chips - chip
+    total = n_group + ns
+    limits = [
+        jnp.where(leading, 19 - 2 * chip, jnp.maximum(0, chip - split - 3)),
+        jnp.where(leading, 22 - 2 * chip, 13),
+        jnp.where(leading, 28 - 2 * chip, 18),
+        total,
+    ]
+    limits = [jnp.clip(limit, 0, total - ns // 2) for limit in limits]
+
+    def noise_part(lo, hi):
         @pl.loop(lo, hi)
-        def _(w):
-            there = chips - 1 - w // steps
-            i = 2 * (steps - 1 - lax.rem(w, steps))
-            offset = first_mode + (there * long + i) * I32(TIME_STEP)
-            h = base[pl.ds(pl.multiple_of(core * half, half), half), :] + offset
-            nz_group[there, i] = noise_of(h)
-            nz_group[there, i + 1] = noise_of(h + I32(TIME_STEP))
-
-    def own_noise(lo, hi):
-        @pl.loop(lo, hi)
-        def _(w):
-            block = w // steps
-            i = lax.rem(w, steps)
-            offset = block * modes * I32(MODE_STEP) + (me_t * steps + i) * I32(TIME_STEP)
-            nz_own[block, i] = noise_of(base[...] + offset)
-
-    n_own = ns * steps
-    early = jnp.where(chip < chips // 2, 200 - 17 * chip, 20)
-    late = jnp.where(chip < chips // 2, 0, n_own // 4)
-    early_group = jnp.minimum(early, n_group)
-    early_own = jnp.minimum(early - early_group, n_own)
-    group_noise(0, early_group)
-    own_noise(0, early_own)
+        def _(u):
+            group = u < n_group
+            there, block = chips - 1 - u, u - n_group
+            start = jnp.where(group, there * long, me_t * steps)
+            mode = jnp.where(group, me_s, block) * modes
+            offset = mode * I32(MODE_STEP) + start * I32(TIME_STEP)
+            stride = jnp.where(group, I32(2 * TIME_STEP), I32(TIME_STEP))
+            at = jnp.where(group, there, chips + block) * steps
+            kind = jnp.where(group, 1, 0)
+
+            @pl.loop(0, steps)
+            def _(i):
+                nz[at + i] = noise_of(base[kind] + (offset + i * stride))
+
+    noise_part(0, limits[0])
 
     def wait_bytes(ref, sem):
         pltpu.make_async_copy(ref, ref, sem).wait()
@@ -143,16 +158,23 @@
     loads[3].wait()
     mine_at = core * chips + chip
     cz[tile(mine_at), :] = coup_ref[...]
-    cs[tile(me_s), :] = coup_ref[...]
-    pl.semaphore_wait(barrier, chips - 1 + 1 + 2 * (ns - 1))
-
-    @pl.loop(0, chips - 1)
-    def _(j):
-        to = j + (j >= chip).astype(I32)
-        pltpu.make_async_remote_copy(
-            src_ref=coup_ref, dst_ref=cz.at[tile(mine_at)], send_sem=send.at[0], recv_sem=recv.at[0],
-            device_id=(2 * to + core, me_s), device_id_type=MESH,
-        ).start()
+    loads[2].wait()
+    inverse_spec = 1.0 / spec_ref[...]
+    fixed[0:steps, :] = coup_ref[...]
+    fixed[steps : 2 * steps, :] = jnp.broadcast_to(inverse_spec, (steps, modes))
+    own_fixed = pl.ds(pl.multiple_of(me_s * long, long), long)
+    cs[own_fixed, :] = fixed[...]
+
+    def to_chips(lo, hi):
+        @pl.loop(lo, hi)
+        def _(to):
+            @pl.when(to != chip)
+            def _():
+                pltpu.make_async_remote_copy(
+                    src_ref=coup_ref, dst_ref=cz.at[tile(mine_at)],
+                    send_sem=send.at[0], recv_sem=recv.at[0],
+                    device_id=(2 * to + core, me_s), device_id_type=MESH,
+                ).start()
 
     def all_copies(make):
         @pl.loop(1, ns)
@@ -161,23 +183,88 @@
 
     def coupling_to_plane(other):
         return pltpu.make_async_remote_copy(
-            src_ref=coup_ref, dst_ref=cs.at[tile(me_s)], send_sem=send.at[1], recv_sem=recv.at[1],
+            src_ref=fixed, dst_ref=cs.at[own_fixed], send_sem=send.at[1], recv_sem=recv.at[1],
             device_id=(me_t, other), device_id_type=MESH,
         )
-
-    all_copies(coupling_to_plane)
 
     def basis_to_plane(other):
         return pltpu.make_async_remote_copy(
-            src_ref=basis_ref.at[pl.ds(pl.multiple_of(other * nodes, nodes), nodes), :],
-            dst_ref=rows.at[me_s], send_sem=send.at[2], recv_sem=recv.at[2],
+            src_ref=basis_ref.at[half_rows(other), :],
+            dst_ref=rows.at[core, me_s], send_sem=send.at[2], recv_sem=recv.at[2],
             device_id=(me_t, other), device_id_type=MESH,
         )
 
-    all_copies(basis_to_plane)
-
-    group_noise(early_group, n_group)
-    own_noise(early_own, jnp.maximum(early_own, n_own - late))
+    def signal_chips(sem, lo, hi):
+        @pl.loop(lo, hi)
+        def _(to):
+            signal(sem, 2 * to + core, me_s)
+
+    @pl.when(leading)
+    def _():
+        pl.semaphore_wait(barrier, split - 1 + 1 + 2 * (ns - 1))
+        to_chips(0, split)
+        all_copies(coupling_to_plane)
+        all_copies(basis_to_plane)
+
+    @pl.when(jnp.logical_not(leading))
+    def _():
+        @pl.when(inner)
+        def _():
+            pl.semaphore_wait(barrier, split)
+
+        @pl.when(chip >= outer)
+        def _():
+            pl.semaphore_wait(barrier, split + 1 + 2 * (ns - 1))
+
+        to_chips(0, split)
+
+        @pl.when(inner)
+        def _():
+            signal(near_in, 2 * (split - 1) + core, me_s)
+
+        signal_chips(line_in, 0, split)
+
+        @pl.when(chip >= outer)
+        def _():
+            all_copies(coupling_to_plane)
+            all_copies(basis_to_plane)
+
+    noise_part(limits[0], limits[1])
+
+    @pl.when(is_hub)
+    def _():
+        pl.semaphore_wait(near_in, outer - split)
+        signal_plane(plane_in)
+
+    @pl.when(inner)
+    def _():
+        pl.semaphore_wait(plane_go, 1)
+        all_copies(coupling_to_plane)
+        all_copies(basis_to_plane)
+
+    noise_part(limits[1], limits[2])
+
+    @pl.when(is_hub)
+    def _():
+        pl.semaphore_wait(plane_in, 1 + 2 * (ns - 1))
+        signal_chips(plane_go, split, outer)
+
+    @pl.when(leading)
+    def _():
+        pl.semaphore_wait(line_in, chips - split)
+
+        @pl.when(chip == 0)
+        def _():
+            signal_chips(line_go, split, chips)
+
+        to_chips(split, chips)
+
+    @pl.when(jnp.logical_not(leading))
+    def _():
+        pl.semaphore_wait(line_go, 1)
+        to_chips(split, chips)
+
+    noise_part(limits[2], limits[3])
 
     wait_bytes(cz.at[pl.ds(0, (chips - 1) * steps)], recv.at[0])
     line = pl.ds(pl.multiple_of(core * chips * steps, steps), chips * steps)
@@ -186,8 +273,6 @@
         device_id=(sibling, me_s), device_id_type=MESH,
     )
     across.start()
-    loads[2].wait()
-    inverse_spec = 1.0 / spec_ref[...]
     across.wait_recv()
 
     c = [
@@ -213,12 +298,11 @@
     above[1] = jnp.where(core == 0, pb, pb + pa * beta[steps])
     mine[0:1, :] = above[0, pl.ds(chip, 1), :]
     mine[1:2, :] = above[1, pl.ds(chip, 1), :]
-    mine[2:steps, :] = jnp.broadcast_to(inverse_spec, (steps - 2, modes))
-    ps[tile(me_s), :] = mine[...]
+    ps[me_s] = mine[...]
 
     def start_to_plane(other):
         return pltpu.make_async_remote_copy(
-            src_ref=mine, dst_ref=ps.at[tile(me_s)], send_sem=send.at[3], recv_sem=recv.at[3],
+            src_ref=mine, dst_ref=ps.at[me_s], send_sem=send.at[3], recv_sem=recv.at[3],
             device_id=(me_t, other), device_id_type=MESH,
         )
 
@@ -256,14 +340,17 @@
             terms = [terms[k] + terms[k + 1] for k in range(0, len(terms), 2)]
         return terms[0]
 
+    def group_at(there, i):
+        return nz[there * steps + i // 2, (i % 2) * half : (i % 2 + 1) * half, :]
+
     def summed(there, carry):
         return carry + added(
-            [omega[i, pl.ds(there, 1), :] * nz_group[there, i] for i in range(long)]
+            [omega[i, pl.ds(there, 1), :] * group_at(there, i) for i in range(long)]
         )
 
     carry_top = lax.fori_loop(chip + 1, chips, summed, jnp.zeros((half, modes), F32))
     carry_low = above[4, pl.ds(chip, 1), :] * carry_top + added(
-        [above[5 + i, pl.ds(chip, 1), :] * nz_group[chip, steps + i] for i in range(steps)]
+        [above[5 + i, pl.ds(chip, 1), :] * group_at(chip, steps + i) for i in range(steps)]
     )
     kin_top = (above[2, pl.ds(chip, 1), :] * carry_top).astype(BF16)
     kin_low = (above[3, pl.ds(chip, 1), :] * carry_low).astype(BF16)
@@ -298,12 +385,21 @@
         low_to_plane(me_s).start()
         kin[slot] = kin_top
 
-    own_noise(jnp.maximum(early_own, n_own - late), n_own)
-
-    wait_bytes(cs.at[pl.ds(0, (ns - 1) * steps)], recv.at[1])
-    wait_bytes(ps.at[pl.ds(0, (ns - 1) * steps)], recv.at[3])
-    c = [cs[pl.ds(i, ns, stride=steps), :] for i in range(steps)]
-    pa, pb, inv_s = [ps[pl.ds(i, ns, stride=steps), :] for i in range(3)]
+    noise_part(limits[3], total)
+
+    wait_bytes(rows.at[0, pl.ds(0, ns - 1)], recv.at[2])
+    loads[4].wait()
+    halves = pltpu.make_async_remote_copy(
+        src_ref=rows.at[core], dst_ref=rows.at[core], send_sem=send.at[6], recv_sem=recv.at[6],
+        device_id=(sibling, me_s), device_id_type=MESH,
+    )
+    halves.start()
+
+    wait_bytes(cs.at[pl.ds(0, (ns - 1) * long)], recv.at[1])
+    wait_bytes(ps.at[pl.ds(0, ns - 1)], recv.at[3])
+    c = [cs[pl.ds(i, ns, stride=long), :] for i in range(steps)]
+    inv_s = cs[pl.ds(steps, ns, stride=long), :]
+    pa, pb = ps[:, 0, :], ps[:, 1, :]
     now = pb + pa
     for i in range(steps):
         pa = pa * (c[i] * c[i])
@@ -315,8 +411,7 @@
             coef_a[i] = kept * c[i + 1]
         now = after
 
-    wait_bytes(rows.at[pl.ds(0, ns - 1)], recv.at[2])
-    loads[4].wait()
+    halves.wait_recv()
     wait_bytes(kin.at[pl.ds(0, 2 * ns - 1)], recv.at[4])
 
     for b in range(ns):
@@ -324,10 +419,10 @@
         for i in range(steps - 1, -1, -1):
             if i < steps - 1:
                 value = coef_a[i, pl.ds(b, 1), :] * value
-            value = value + coef_s[i, pl.ds(b, 1), :] * nz_own[b, i]
+            value = value + coef_s[i, pl.ds(b, 1), :] * nz[(chips + b) * steps + i]
             vals[b, pl.ds(i * vecs, vecs), :] = value.astype(BF16)
         product = lax.dot_general(
-            rows[b], vals[b], (((1,), (1,)), ((), ())), preferred_element_type=F32
+            jnp.concatenate([rows[0, b], rows[1, b]], axis=0), vals[b], (((1,), (1,)), ((), ())), preferred_element_type=F32
         )
         if b == 0:
             out_ref[...] = product
@@ -335,9 +430,10 @@
             out_ref[...] += product
 
     wait_bytes(cz.at[pl.ds(0, (chips - 1) * steps)], send.at[0])
-    wait_bytes(cs.at[pl.ds(0, (ns - 1) * steps)], send.at[1])
-    wait_bytes(rows.at[pl.ds(0, ns - 1)], send.at[2])
-    wait_bytes(ps.at[pl.ds(0, (ns - 1) * steps)], send.at[3])
+    wait_bytes(cs.at[pl.ds(0, (ns - 1) * long)], send.at[1])
+    wait_bytes(rows.at[0, pl.ds(0, ns - 1)], send.at[2])
+    halves.wait_send()
+    wait_bytes(ps.at[pl.ds(0, ns - 1)], send.at[3])
     wait_bytes(kin.at[pl.ds(0, 2 * ns - 1)], send.at[4])
     across.wait_send()
 
@@ -360,23 +456,24 @@
                 smem((vecs,), I32),
                 vmem((1, modes), F32),
                 vmem((steps, modes), F32),
-                vmem((vecs, modes), I32),
+                vmem((2, vecs, modes), I32),
+                vmem((2 * steps, modes), F32),
                 vmem((zt * steps, modes), F32),
-                vmem((ns * steps, modes), F32),
-                vmem((ns * steps, modes), F32),
-                vmem((ns, nodes, modes), BF16),
+                vmem((2 * steps * ns, modes), F32),
+                vmem((ns, 2, modes), F32),
+                vmem((2, ns, nodes // 2, modes), BF16),
                 vmem((2 * ns + 2, vecs // 2, modes), BF16),
-                vmem((steps, modes), F32),
-                vmem((zt // 2, 2 * steps, vecs // 2, modes), F32),
-                vmem((ns, steps, vecs, modes), F32),
+                vmem((2, modes), F32),
+                vmem(((zt // 2 + ns) * steps, vecs, modes), F32),
                 vmem((2 * steps, zt // 2, modes), F32),
                 vmem((5 + steps, zt // 2, modes), F32),
                 vmem((steps, ns, modes), F32),
                 vmem((steps, ns, modes), F32),
                 vmem((ns, steps * vecs, modes), BF16),
-                pltpu.SemaphoreType.DMA((6,)),
-                pltpu.SemaphoreType.DMA((6,)),
+                pltpu.SemaphoreType.DMA((7,)),
+                pltpu.SemaphoreType.DMA((7,)),
                 pltpu.SemaphoreType.DMA((5,)),
+                pltpu.SemaphoreType.REGULAR((5,)),
             ],
             compiler_params=pltpu.CompilerParams(
                 collective_id=0, has_side_effects=True, vmem_limit_bytes=62 * 2**20

time: 37.3 us -> 35.5 us (0.952)
  the two profiles are of different devices: /device:TPU:1 before, /device:TPU:480 now
where the time goes in v3:
time: 35.5 us; the launch traced here: 35.3 us
  Pallas kernels  33.6 us (95%)
  local copies, waits for them, and re-layouts  1.67 us (5%)
    pallas_call x1, Pallas kernels, local(): pl.pallas_call(functools.partial(kernel, zt, ns, steps, vecs), out_shape=...  33.6 us
    unnamed x1, local copies, waits for them, and re-layouts  1.67 us

profile of v3, /device:TPU:480, one launch (start us, length us, event | category | flops | bytes accessed | tf_op | source)
XLA Modules:
  0.0 35.3 jit_solution(9415934831066244479)
XLA Ops:
  0.0 33.6 %shard_map.55 = f32[128,512]{1,0:T(8,128)} custom-call(s32[64]{0:T(128)} %keys_hbm.1, s32[64]{0:T(128)} %counters_hbm.1, f32[1,128]{1,0:T(1,128)} %bitcast.1, f32[8,128]{1,0:T(8,128)} %coup_hbm.1, bf16[2048,128]{1,0:T(8,128)(2,1)} %basis_ref.1), custom_call_target="tpu_custom_call" | custom-call | tf_op jit(solution)/shard_map/pallas_call | solution.py:449
  33.6 1.7 %copy.7 = f32[128,512]{1,0:T(8,128)} copy(f32[128,512]{1,0:T(8,128)} %shard_map.55) | data formatting | bytes 524288

commit v4 on v3

--- a/solution.py
+++ b/solution.py
@@ -64,7 +64,7 @@
 
     split, outer = chips // 2, chips * 3 // 4
     leading = chip < split
-    inner = jnp.logical_and(chip >= split, chip < outer)
+    third = jnp.logical_and(chip >= split, chip < outer)
     is_hub = chip == split - 1
     line_in, near_in, plane_in, line_go, plane_go = (meet.at[k] for k in range(5))
     barrier = pltpu.get_barrier_semaphore()
@@ -87,9 +87,17 @@
         def _(j):
             signal(barrier, lax.rem(me_t + 2 * j, zt), me_s)
 
-    @pl.when(jnp.logical_not(inner))
+    @pl.when(jnp.logical_not(third))
     def _():
         signal_plane(barrier)
+
+    @pl.when(chip >= outer)
+    def _():
+        @pl.loop(outer, chips)
+        def _(to):
+            @pl.when(to != chip)
+            def _():
+                signal(barrier, 2 * to + core, me_s)
 
     def half_rows(owner):
         start = owner * nodes + core * (nodes // 2)
@@ -165,14 +173,14 @@
     own_fixed = pl.ds(pl.multiple_of(me_s * long, long), long)
     cs[own_fixed, :] = fixed[...]
 
-    def to_chips(lo, hi):
+    def to_chips(lo, hi, k=0):
         @pl.loop(lo, hi)
         def _(to):
             @pl.when(to != chip)
             def _():
                 pltpu.make_async_remote_copy(
                     src_ref=coup_ref, dst_ref=cz.at[tile(mine_at)],
-                    send_sem=send.at[0], recv_sem=recv.at[0],
+                    send_sem=send.at[0], recv_sem=recv.at[k],
                     device_id=(2 * to + core, me_s), device_id_type=MESH,
                 ).start()
 
@@ -194,6 +202,10 @@
             device_id=(me_t, other), device_id_type=MESH,
         )
 
+    def passed_on(side):
+        count = (outer - split) * steps
+        return cz.at[pl.ds(pl.multiple_of((side * chips + split) * steps, steps), count)]
+
     def signal_chips(sem, lo, hi):
         @pl.loop(lo, hi)
         def _(to):
@@ -208,24 +220,25 @@
 
     @pl.when(jnp.logical_not(leading))
     def _():
-        @pl.when(inner)
+        @pl.when(third)
         def _():
             pl.semaphore_wait(barrier, split)
 
         @pl.when(chip >= outer)
         def _():
-            pl.semaphore_wait(barrier, split + 1 + 2 * (ns - 1))
-
-        to_chips(0, split)
-
-        @pl.when(inner)
+            pl.semaphore_wait(barrier, split + chips - outer - 1 + 1 + 2 * (ns - 1))
+
+        @pl.when(third)
         def _():
+            to_chips(0, split, 7)
             signal(near_in, 2 * (split - 1) + core, me_s)
 
         signal_chips(line_in, 0, split)
 
         @pl.when(chip >= outer)
         def _():
+            to_chips(0, split)
+            to_chips(outer, chips)
             all_copies(coupling_to_plane)
             all_copies(basis_to_plane)
 
@@ -236,9 +249,10 @@
         pl.semaphore_wait(near_in, outer - split)
         signal_plane(plane_in)
 
-    @pl.when(inner)
+    @pl.when(third)
     def _():
         pl.semaphore_wait(plane_go, 1)
+        to_chips(split, outer)
         all_copies(coupling_to_plane)
         all_copies(basis_to_plane)
 
@@ -255,18 +269,36 @@
 
         @pl.when(chip == 0)
         def _():
-            signal_chips(line_go, split, chips)
+            signal_chips(line_go, outer, chips)
 
         to_chips(split, chips)
+        wait_bytes(passed_on(0), recv.at[7])
+
+    @pl.when(chip == 0)
+    def _():
+        @pl.loop(outer, chips)
+        def _(to):
+            pltpu.make_async_remote_copy(
+                src_ref=passed_on(core), dst_ref=passed_on(core),
+                send_sem=send.at[7], recv_sem=recv.at[0],
+                device_id=(2 * to + core, me_s), device_id_type=MESH,
+            ).start()
+
+    @pl.when(chip >= outer)
+    def _():
+        pl.semaphore_wait(line_go, 1)
+        to_chips(split, outer)
+
+    noise_part(limits[2], limits[3])
+
+    @pl.when(leading)
+    def _():
+        wait_bytes(cz.at[pl.ds(0, (chips - 1 - outer + split) * steps)], recv.at[0])
 
     @pl.when(jnp.logical_not(leading))
     def _():
-        pl.semaphore_wait(line_go, 1)
-        to_chips(split, chips)
-
-    noise_part(limits[2], limits[3])
-
-    wait_bytes(cz.at[pl.ds(0, (chips - 1) * steps)], recv.at[0])
+        wait_bytes(cz.at[pl.ds(0, (chips - 1) * steps)], recv.at[0])
+
     line = pl.ds(pl.multiple_of(core * chips * steps, steps), chips * steps)
     across = pltpu.make_async_remote_copy(
         src_ref=cz.at[line], dst_ref=cz.at[line], send_sem=send.at[5], recv_sem=recv.at[5],
@@ -429,7 +461,18 @@
         else:
             out_ref[...] += product
 
-    wait_bytes(cz.at[pl.ds(0, (chips - 1) * steps)], send.at[0])
+    @pl.when(third)
+    def _():
+        wait_bytes(cz.at[pl.ds(0, (outer - 1) * steps)], send.at[0])
+
+    @pl.when(jnp.logical_not(third))
+    def _():
+        wait_bytes(cz.at[pl.ds(0, (chips - 1) * steps)], send.at[0])
+
+    @pl.when(chip == 0)
+    def _():
+        wait_bytes(cz.at[pl.ds(0, (chips - outer) * (outer - split) * steps)], send.at[7])
+
     wait_bytes(cs.at[pl.ds(0, (ns - 1) * long)], send.at[1])
     wait_bytes(rows.at[0, pl.ds(0, ns - 1)], send.at[2])
     halves.wait_send()
@@ -470,8 +513,8 @@
                 vmem((steps, ns, modes), F32),
                 vmem((steps, ns, modes), F32),
                 vmem((ns, steps * vecs, modes), BF16),
-                pltpu.SemaphoreType.DMA((7,)),
-                pltpu.SemaphoreType.DMA((7,)),
+                pltpu.SemaphoreType.DMA((8,)),
+                pltpu.SemaphoreType.DMA((8,)),
                 pltpu.SemaphoreType.DMA((5,)),
                 pltpu.SemaphoreType.REGULAR((5,)),
             ],

time: 35.5 us -> 32.9 us (0.927)
  the two profiles are of different devices: /device:TPU:480 before, /device:TPU:1 now
where the time goes in v4:
time: 32.9 us; the launch traced here: 32.7 us
  Pallas kernels  31 us (94%)
  local copies, waits for them, and re-layouts  1.67 us (5%)
    pallas_call x1, Pallas kernels, local(): pl.pallas_call(functools.partial(kernel, zt, ns, steps, vecs), out_shape=...  31 us
    unnamed x1, local copies, waits for them, and re-layouts  1.67 us

profile of v4, /device:TPU:1, one launch (start us, length us, event | category | flops | bytes accessed | tf_op | source)
XLA Modules:
  0.0 32.7 jit_solution(9310681952759824372)
XLA Ops:
  0.0 31.0 %shard_map.55 = f32[128,512]{1,0:T(8,128)} custom-call(s32[64]{0:T(128)} %keys_hbm.1, s32[64]{0:T(128)} %counters_hbm.1, f32[1,128]{1,0:T(1,128)} %bitcast.1, f32[8,128]{1,0:T(8,128)} %coup_hbm.1, bf16[2048,128]{1,0:T(8,128)(2,1)} %basis_ref.1), custom_call_target="tpu_custom_call" | custom-call | tf_op jit(solution)/shard_map/pallas_call | solution.py:492
  31.0 1.7 %copy.7 = f32[128,512]{1,0:T(8,128)} copy(f32[128,512]{1,0:T(8,128)} %shard_map.55) | data formatting | bytes 524288

commit v5 on v4

--- a/solution.py
+++ b/solution.py
@@ -51,7 +51,7 @@
     keys_hbm, counters_hbm, spec_hbm, coup_hbm, basis_ref, out_ref,
     keys_ref, counters_ref, spec_ref, coup_ref, base, fixed, cz, cs, ps, rows, kin, mine,
     nz, omega, above, coef_s, coef_a, vals,
-    send, recv, local_sem, meet,
+    send, recv, local_sem, meet, arrived,
 ):
     modes = coup_ref.shape[1]
     nodes = basis_ref.shape[0] // ns
@@ -68,6 +68,17 @@
     is_hub = chip == split - 1
     line_in, near_in, plane_in, line_go, plane_go = (meet.at[k] for k in range(5))
     barrier = pltpu.get_barrier_semaphore()
+
+    side = 4 if ns == 16 else 1
+    wide = ns // side
+    offsets = sorted(
+        ((dx, dy) for dx in range(side) for dy in range(wide) if dx or dy),
+        key=lambda d: -min(d[0], side - d[0]) - min(d[1], wide - d[1]),
+    )
+
+    def partner(d):
+        x, y = me_s // wide, lax.rem(me_s, wide)
+        return lax.rem(x + d[0], side) * wide + lax.rem(y + d[1], wide)
 
     def signal(sem, t, s):
         pl.semaphore_signal(sem, inc=1, device_id=(t, s), device_id_type=MESH)
@@ -381,40 +392,48 @@
         )
 
     carry_top = lax.fori_loop(chip + 1, chips, summed, jnp.zeros((half, modes), F32))
+    kin_top = (above[2, pl.ds(chip, 1), :] * carry_top).astype(BF16)
+    slot = 2 * me_s + core
+
+    out_low, out_top = kin.at[2 * ns], kin.at[2 * ns + 1]
+    out_top[...] = kin_top
+
+    def to_plane(source, t, other):
+        return pltpu.make_async_remote_copy(
+            src_ref=source, dst_ref=kin.at[slot], send_sem=send.at[4], recv_sem=arrived.at[me_s],
+            device_id=(t, other), device_id_type=MESH,
+        )
+
+    @pl.when(chip == 0)
+    def _():
+        for d in offsets:
+            to_plane(out_top, 2 * chip + 1, partner(d)).start()
+
     carry_low = above[4, pl.ds(chip, 1), :] * carry_top + added(
         [above[5 + i, pl.ds(chip, 1), :] * group_at(chip, steps + i) for i in range(steps)]
     )
-    kin_top = (above[2, pl.ds(chip, 1), :] * carry_top).astype(BF16)
     kin_low = (above[3, pl.ds(chip, 1), :] * carry_low).astype(BF16)
-    slot = 2 * me_s + core
-
-    out_low, out_top = kin.at[2 * ns], kin.at[2 * ns + 1]
     out_low[...] = kin_low
-    out_top[...] = kin_top
-
-    def low_to_plane(other):
-        return pltpu.make_async_remote_copy(
-            src_ref=out_low, dst_ref=kin.at[slot], send_sem=send.at[4], recv_sem=recv.at[4],
-            device_id=(2 * chip, other), device_id_type=MESH,
-        )
-
-    def top_to_plane(other):
-        return pltpu.make_async_remote_copy(
-            src_ref=out_top, dst_ref=kin.at[slot], send_sem=send.at[4], recv_sem=recv.at[4],
-            device_id=(2 * chip + 1, other), device_id_type=MESH,
-        )
-
-    all_copies(low_to_plane)
-    all_copies(top_to_plane)
+
+    @pl.when(chip == 0)
+    def _():
+        for d in offsets:
+            to_plane(out_low, 2 * chip, partner(d)).start()
+
+    @pl.when(chip > 0)
+    def _():
+        for d in offsets:
+            to_plane(out_top, 2 * chip + 1, partner(d)).start()
+            to_plane(out_low, 2 * chip, partner(d)).start()
 
     @pl.when(core == 0)
     def _():
-        top_to_plane(me_s).start()
+        to_plane(out_top, sibling, me_s).start()
         kin[slot] = kin_low
 
     @pl.when(core == 1)
     def _():
-        low_to_plane(me_s).start()
+        to_plane(out_low, sibling, me_s).start()
         kin[slot] = kin_top
 
     noise_part(limits[3], total)
@@ -444,9 +463,14 @@
         now = after
 
     halves.wait_recv()
-    wait_bytes(kin.at[pl.ds(0, 2 * ns - 1)], recv.at[4])
-
-    for b in range(ns):
+
+    order = [(0, 0), *offsets]
+    blocks = [partner(d) if k else me_s for k, d in enumerate(order)]
+    stops = [ns * g // 2 for g in range(2 + 1)]
+    for k, b in enumerate(blocks):
+        if k in stops:
+            for q in range(k, stops[stops.index(k) + 1]):
+                wait_bytes(kin.at[pl.ds(0, 2 if q else 1)], arrived.at[blocks[q]])
         value = jnp.concatenate([kin[2 * b], kin[2 * b + 1]], axis=0).astype(F32)
         for i in range(steps - 1, -1, -1):
             if i < steps - 1:
@@ -456,7 +480,7 @@
         product = lax.dot_general(
             jnp.concatenate([rows[0, b], rows[1, b]], axis=0), vals[b], (((1,), (1,)), ((), ())), preferred_element_type=F32
         )
-        if b == 0:
+        if k == 0:
             out_ref[...] = product
         else:
             out_ref[...] += product
@@ -517,6 +541,7 @@
                 pltpu.SemaphoreType.DMA((8,)),
                 pltpu.SemaphoreType.DMA((5,)),
                 pltpu.SemaphoreType.REGULAR((5,)),
+                pltpu.SemaphoreType.DMA((ns,)),
             ],
             compiler_params=pltpu.CompilerParams(
                 collective_id=0, has_side_effects=True, vmem_limit_bytes=62 * 2**20

time: 32.9 us -> 32.9 us (level)
  no operation moved by 1% of the time
where the time goes in v5:
time: 32.9 us; the launch traced here: 32.7 us
  Pallas kernels  31 us (94%)
  local copies, waits for them, and re-layouts  1.67 us (5%)
    pallas_call x1, Pallas kernels, local(): pl.pallas_call(functools.partial(kernel, zt, ns, steps, vecs), out_shape=...  31 us
    unnamed x1, local copies, waits for them, and re-layouts  1.67 us

profile of v5, /device:TPU:1, one launch (start us, length us, event | category | flops | bytes accessed | tf_op | source)
XLA Modules:
  0.0 32.7 jit_solution(8919335418836184705)
XLA Ops:
  0.0 31.0 %shard_map.55 = f32[128,512]{1,0:T(8,128)} custom-call(s32[64]{0:T(128)} %keys_hbm.1, s32[64]{0:T(128)} %counters_hbm.1, f32[1,128]{1,0:T(1,128)} %bitcast.1, f32[8,128]{1,0:T(8,128)} %coup_hbm.1, bf16[2048,128]{1,0:T(8,128)(2,1)} %basis_ref.1), custom_call_target="tpu_custom_call" | custom-call | tf_op jit(solution)/shard_map/pallas_call | solution.py:516
  31.0 1.7 %copy.7 = f32[128,512]{1,0:T(8,128)} copy(f32[128,512]{1,0:T(8,128)} %shard_map.55) | data formatting | bytes 524288

commit v6 on v4

--- a/solution.py
+++ b/solution.py
@@ -404,8 +404,8 @@
             device_id=(2 * chip + 1, other), device_id_type=MESH,
         )
 
+    all_copies(top_to_plane)
     all_copies(low_to_plane)
-    all_copies(top_to_plane)
 
     @pl.when(core == 0)
     def _():

time: 32.9 us -> 32.7 us (level)
  no operation moved by 1% of the time
where the time goes in v6:
time: 32.7 us; the launch traced here: 32.5 us
  Pallas kernels  30.8 us (94%)
  local copies, waits for them, and re-layouts  1.67 us (5%)
    pallas_call x1, Pallas kernels, local(): pl.pallas_call(functools.partial(kernel, zt, ns, steps, vecs), out_shape=...  30.8 us
    unnamed x1, local copies, waits for them, and re-layouts  1.67 us

profile of v6, /device:TPU:1, one launch (start us, length us, event | category | flops | bytes accessed | tf_op | source)
XLA Modules:
  0.0 32.5 jit_solution(17867278233679009643)
XLA Ops:
  0.0 30.8 %shard_map.55 = f32[128,512]{1,0:T(8,128)} custom-call(s32[64]{0:T(128)} %keys_hbm.1, s32[64]{0:T(128)} %counters_hbm.1, f32[1,128]{1,0:T(1,128)} %bitcast.1, f32[8,128]{1,0:T(8,128)} %coup_hbm.1, bf16[2048,128]{1,0:T(8,128)(2,1)} %basis_ref.1), custom_call_target="tpu_custom_call" | custom-call | tf_op jit(solution)/shard_map/pallas_call | solution.py:492
  30.8 1.7 %copy.7 = f32[128,512]{1,0:T(8,128)} copy(f32[128,512]{1,0:T(8,128)} %shard_map.55) | data formatting | bytes 524288
